TPU v7x, 256 devices: a whole 4x4x8 slice. The times are simulated.
256 devices in a mesh: replica: 32 (over x, z_hi, core), fsdp: 8 (over y, z_lo).
Axes of the slice: x: 4, y: 4, z: 8 (z_hi: 4, z_lo: 2; z = z_hi * 2 + z_lo), core: 2. Of those that a mesh axis runs over, the one named last changes fastest.
Arguments:
- tokens: bfloat16 [65536, 8192], P(('replica', 'fsdp')), may hold values from -6 to 6
- cotangent: bfloat16 [65536, 512], P(('replica', 'fsdp')), may hold values from -0.125 to 0.125
- gain: float32 [32, 8192], P('replica'), may hold values from 0.1 to 1.9
- value_weight: bfloat16 [32, 8192, 512], P('replica', 'fsdp'), may hold values from -0.25 to 0.25
- fragment: bfloat16 [32, 8192, 1024], P('replica', 'fsdp'), may hold values from -6 to 6
- global_table: float32 [4, 8192, 1024], P(None, ('fsdp', 'replica')), may hold values from -6 to 6
- momentum_table: float32 [4, 8192, 1024], P(None, ('fsdp', 'replica')), may hold values from -4 to 4
- frag_index: int32 [], replicated, may hold values from 0 to 3
Outputs:
- weight_grad: bfloat16 [32, 8192, 512], P('replica', 'fsdp')
- gain_grad: float32 [32, 8192], P('replica')
- new_fragment: bfloat16 [32, 8192, 1024], P('replica', 'fsdp')
- new_global: float32 [4, 8192, 1024], P(None, ('fsdp', 'replica'))
- new_momentum: float32 [4, 8192, 1024], P(None, ('fsdp', 'replica'))
All inputs are finite; a program needn't handle non-finite values.
Results may differ from a plain program's by a relative error of at most 0.017.
Values may be sent and summed in bfloat16 or wider, within the bound.
A program may use at most 128 MiB of HBM per device.

v0:
```python
import jax
import jax.numpy as jnp
from jax import lax
from jax.sharding import PartitionSpec as P

epsilon = 1e-05
outer_rate = 0.7
outer_beta = 0.9
mix_weight = 0.5


def body(tokens, cotangent, gain, value_weight, fragment, global_table, momentum_table, frag_index):
    gains = gain[0]
    weight = value_weight[0]
    floats = tokens.astype(jnp.float32)
    inverse = lax.rsqrt(jnp.mean(floats * floats, axis=-1, keepdims=True) + epsilon)
    normed = floats * inverse
    scaled = (normed * gains).astype(jnp.bfloat16)
    back = lax.dot_general(
        cotangent,
        lax.all_gather(weight, "fsdp", axis=0, tiled=True),
        (((1,), (1,)), ((), ())),
        preferred_element_type=jnp.float32,
    )
    columns = normed
    partial_gain = jnp.sum(columns * back, axis=0)
    gain_grad = lax.psum(partial_gain, "fsdp")
    columns = scaled
    weight_grad = lax.psum_scatter(
        lax.dot_general(
            columns, cotangent, (((0,), (0,)), ((), ())), preferred_element_type=jnp.float32
        ).astype(jnp.bfloat16),
        "fsdp",
        scatter_dimension=0,
        tiled=True,
    )
    chosen = lax.dynamic_index_in_dim(global_table, frag_index, 0, keepdims=False)
    velocity = lax.dynamic_index_in_dim(momentum_table, frag_index, 0, keepdims=False)
    local = fragment[0].astype(jnp.float32)
    replicas = lax.axis_size("replica")
    summed = lax.psum_scatter(
        local.astype(jnp.bfloat16), "replica", scatter_dimension=0, tiled=True
    ).astype(jnp.float32)
    delta = chosen - summed / replicas
    new_velocity = outer_beta * velocity + delta
    new_params = chosen - outer_rate * (delta + outer_beta * new_velocity)
    full_params = lax.all_gather(new_params, "replica", axis=0, tiled=True)
    new_fragment = (mix_weight * local + (1.0 - mix_weight) * full_params).astype(jnp.bfloat16)[
        None
    ]
    new_global = lax.dynamic_update_index_in_dim(global_table, new_params, frag_index, 0)
    new_momentum = lax.dynamic_update_index_in_dim(momentum_table, new_velocity, frag_index, 0)
    return (weight_grad[None], gain_grad[None], new_fragment, new_global, new_momentum)


def solution(mesh):
    placed = (
        P(("replica", "fsdp"), None),
        P(("replica", "fsdp"), None),
        P("replica", None),
        P("replica", "fsdp", None),
        P("replica", "fsdp", None),
        P(None, ("fsdp", "replica"), None),
        P(None, ("fsdp", "replica"), None),
        P(),
    )
    return jax.shard_map(
        body,
        mesh=mesh,
        in_specs=placed,
        out_specs=(
            P("replica", "fsdp", None),
            P("replica", None),
            P("replica", "fsdp", None),
            P(None, ("fsdp", "replica"), None),
            P(None, ("fsdp", "replica"), None),
        ),
        check_vma=False,
    )
```

profile of v0, /device:TPU:1, one launch (start us, length us, event | category | flops | bytes accessed | tf_op | source)
XLA Modules:
  0.0 521.8 jit_solution(3852087064441866261)
XLA Ops:
  7.2 0.0 copy-start
  7.2 0.0 copy-start.5
  7.2 0.0 reduce-scatter.5.cloned.1.call-start
  7.2 1.1 copy.18
  8.3 1.0 copy.19
  9.4 0.0 reduce-scatter.5.cloned.1.call-update
  9.4 0.0 all-gather.4.cloned.1.call-start
  10.1 95.1 %reduce-scatter.5.cloned.1.call-done = bf16[32,1024]{1,0:T(8,128)(2,1)} async-done(((bf16[1024,1024]{1,0:T(8,128)(2,1)}), bf16[32,1024]{1,0:T(8,128)(2,1)}) %reduce-scatter.5.cloned.1.call-update) | async-done | bytes 65552 | tf_op jit(solution)/shard_map/reduce_scatter | solution.py:41
  105.2 1.6 bitcast_subtract_fusion
  106.8 0.0 all-gather.4.cloned.1.call-update
  106.8 0.0 all-gather.6.cloned.1.call-start
  106.9 0.7 all-gather.6.cloned.1.call-update
  107.5 0.0 reduce-scatter.3.cloned.1.call-start
  107.6 3.1 fusion.2
  110.7 0.0 copy-done
  110.7 0.0 copy-done.5
  110.7 8.1 %convolution_convert_fusion = bf16[8192,512]{1,0:T(8,128)(2,1)} fusion(bf16[256,512]{1,0:T(8,128)(2,1)S(1)} %copy-done, bf16[256,8192]{1,0:T(8,128)(2,1)} %param.8, f32[8192]{0:T(1024)S(1)} %bitcast.32, f32[256]{0:T(256)S(1)} %add_rsqrt_fusion), kind=kOutput, calls=%fused_computation | convolution fusion | flops 2160066560 | bytes 12878848 | tf_op jit(solution)/shard_map/dot_general | solution.py:30
  118.9 0.0 copy-start.2
  118.9 0.0 reduce-scatter.3.cloned.1.call-update
  118.9 0.9 copy-done.2
  119.8 0.9 bitcast_dynamic-update-slice_fusion
  120.7 0.0 copy-start.3
  120.7 0.0 copy-start.4
  120.7 48.0 %all-gather.4.cloned.1.call-done = f32[1024,1024]{1,0:T(8,128)} async-done(((f32[32,1024]{1,0:T(8,128)}), f32[1024,1024]{1,0:T(8,128)}) %all-gather.4.cloned.1.call-update) | async-done | bytes 4194320 | tf_op jit(solution)/shard_map/all_gather | solution.py:47
  168.8 0.0 copy-done.1
  168.8 4.3 fusion.7
  173.1 165.6 %all-gather.6.cloned.1.call-done = bf16[1,8192,512]{2,1,0:T(8,128)(2,1)} async-done(((bf16[1,1024,512]{2,1,0:T(8,128)(2,1)}), bf16[1,8192,512]{2,1,0:T(8,128)(2,1)}) %all-gather.6.cloned.1.call-update) | async-done | bytes 8388624 | tf_op jit(solution)/shard_map/all_gather | solution.py:21
  338.6 7.0 %fusion.8 = f32[8192]{0:T(1024)S(1)} fusion(bf16[256,512]{1,0:T(8,128)(2,1)S(1)} %copy-done, bf16[1,8192,512]{2,1,0:T(8,128)(2,1)} %all-gather.6.cloned.1.call-done, f32[256]{0:T(256)S(1)} %add_rsqrt_fusion, bf16[256,8192]{1,0:T(8,128)(2,1)} %param.8), kind=kOutput, calls=%fused_computation.12 | convolution fusion | flops 2155864064 | bytes 12878848 | tf_op jit(solution)/shard_map/dot_general | solution.py:19
  345.6 0.0 copy-done.3
  345.6 0.0 copy-done.4
  345.6 27.4 %psum.7 = f32[1,8192]{1,0:T(1,128)} all-reduce(f32[1,8192]{1,0:T(1,128)S(1)} %bitcast.30), channel_id=1, replica_groups=mesh['replica'=32,'fsdp'=8] {'fsdp'}, use_global_device_ids=true, to_apply=%region_3.0 | all-reduce | flops 8192 | bytes 65536 | tf_op jit(solution)/shard_map/psum | solution.py:27
  373.0 142.2 %reduce-scatter.3.cloned.1.call-done = bf16[1024,512]{1,0:T(8,128)(2,1)} async-done(((bf16[8192,512]{1,0:T(8,128)(2,1)}), bf16[1024,512]{1,0:T(8,128)(2,1)}) %reduce-scatter.3.cloned.1.call-update) | async-done | bytes 1048592 | tf_op jit(solution)/shard_map/reduce_scatter | solution.py:29
  (2 shorter events, 0.0 us)
Async XLA Ops:
  7.2 103.5 %copy-start = (bf16[256,512]{1,0:T(8,128)(2,1)S(1)}, bf16[256,512]{1,0:T(8,128)(2,1)}, u32[]{:S(2)}) copy-start(bf16[256,512]{1,0:T(8,128)(2,1)} %param.9) | copy-start | bytes 786436
  7.2 103.5 %copy-start.5 = (f32[1,8192]{1,0:T(1,128)S(1)}, f32[1,8192]{1,0:T(1,128)}, u32[]{:S(2)}) copy-start(f32[1,8192]{1,0:T(1,128)} %param.10) | copy-start | bytes 98308
  7.2 98.0 %reduce-scatter.5.cloned.1.call-start = ((), (), s32[]{:S(2)}) async-start(), calls=%async_computation.3 | async-start | bytes 2162688 | tf_op jit(solution)/shard_map/reduce_scatter | solution.py:41
  9.4 159.4 %all-gather.4.cloned.1.call-start = ((), (), s32[]{:S(2)}) async-start(), calls=%async_computation.4 | async-start | bytes 4325376 | tf_op jit(solution)/shard_map/all_gather | solution.py:47
  106.8 231.8 %all-gather.6.cloned.1.call-start = ((), (), s32[]{:S(2)}) async-start(), calls=%async_computation.5 | async-start | bytes 9437184 | tf_op jit(solution)/shard_map/all_gather | solution.py:21
  107.5 407.7 %reduce-scatter.3.cloned.1.call-start = ((), (), s32[]{:S(2)}) async-start(), calls=%async_computation.2 | async-start | bytes 9437184 | tf_op jit(solution)/shard_map/reduce_scatter | solution.py:29
  118.9 0.9 copy-start.2
  118.9 49.9 %copy-start.1 = (bf16[1,1024,1024]{2,1,0:T(8,128)(2,1)S(1)}, bf16[1,1024,1024]{2,1,0:T(8,128)(2,1)}, u32[]{:S(2)}) copy-start(bf16[1,1024,1024]{2,1,0:T(8,128)(2,1)} %param.12) | copy-start | bytes 6291460
  120.7 224.9 %copy-start.3 = (f32[4,32,1024]{2,1,0:T(8,128)}, f32[4,32,1024]{2,1,0:T(8,128)S(1)}, u32[]{:S(2)}) copy-start(f32[4,32,1024]{2,1,0:T(8,128)S(1)} %get-tuple-element.8) | copy-start | bytes 1572868
  120.7 224.9 %copy-start.4 = (f32[4,32,1024]{2,1,0:T(8,128)}, f32[4,32,1024]{2,1,0:T(8,128)S(1)}, u32[]{:S(2)}) copy-start(f32[4,32,1024]{2,1,0:T(8,128)S(1)} %get-tuple-element.7) | copy-start | bytes 1572868
Sparse Core Ops, SparseCore 0:
  11.9 93.3 reduce-scatter.4
  108.3 60.3 all-gather.3
  170.6 167.9 all-gather.5
  341.6 173.5 reduce-scatter.2
where the time goes:
time: 522 us
  waiting for transfers between devices  452 us (87%)
  blocking collectives  27.4 us (5%)
  matrix products  15.1 us (3%)
  between operations  14.5 us (3%)
  other arithmetic  8.97 us (2%)
    all_gather x1, waiting for transfers between devices, body(): lax.all_gather(weight, 'fsdp', axis=0, tiled=True)  166 us
    reduce_scatter x1, waiting for transfers between devices, body(): lax.psum_scatter(lax.dot_general(columns, cotangent, (((0,), (0,)), ((),...  142 us
    reduce_scatter x1, waiting for transfers between devices, body(): lax.psum_scatter(local.astype(jnp.bfloat16), 'replica', scatter_dimension...  95.1 us
    all_gather x1, waiting for transfers between devices, body(): full_params = lax.all_gather(new_params, 'replica', axis=0, tiled=True)  48 us
    psum x1, blocking collectives, body(): gain_grad = lax.psum(partial_gain, 'fsdp')  27.4 us
  transfers between devices with their start and end apart: 4, of which 4 were waited for; matrix products, arithmetic and copies ran while one was open for 4% of the time, Pallas kernels for 0%

commit v1 on v0

--- a/solution.py
+++ b/solution.py
@@ -24,7 +24,8 @@
     )
     columns = normed
     partial_gain = jnp.sum(columns * back, axis=0)
-    gain_grad = lax.psum(partial_gain, "fsdp")
+    terms = lax.all_gather(partial_gain, "fsdp", axis=0, tiled=False)
+    gain_grad = terms.sum(axis=0)
     columns = scaled
     weight_grad = lax.psum_scatter(
         lax.dot_general(

time: 522 us -> 524 us (level)
    psum x1 -> x0, blocking collectives: 27.4 us -> none  [body(): gain_grad = lax.psum(partial_gain, 'fsdp')]
    all_gather x0 -> x1, blocking collectives: none -> 24.1 us  [body(): terms = lax.all_gather(partial_gain, 'fsdp', axis=0, tiled=False)]
  transfers between devices with their start and end apart: 4 -> 4, of which waited for: 4 -> 4; matrix products, arithmetic and copies ran while one was open for 4% -> 5% of each run, Pallas kernels for 0% -> 0%
where the time goes in v1:
time: 524 us
  waiting for transfers between devices  457 us (87%)
  blocking collectives  24.1 us (5%)
  matrix products  15.1 us (3%)
  between operations  14.5 us (3%)
  other arithmetic  9.65 us (2%)
    all_gather x1, waiting for transfers between devices, body(): lax.all_gather(weight, 'fsdp', axis=0, tiled=True)  166 us
    reduce_scatter x1, waiting for transfers between devices, body(): lax.psum_scatter(lax.dot_general(columns, cotangent, (((0,), (0,)), ((),...  147 us
    reduce_scatter x1, waiting for transfers between devices, body(): lax.psum_scatter(local.astype(jnp.bfloat16), 'replica', scatter_dimension...  95.1 us
    all_gather x1, waiting for transfers between devices, body(): full_params = lax.all_gather(new_params, 'replica', axis=0, tiled=True)  48 us
    all_gather x1, blocking collectives, body(): terms = lax.all_gather(partial_gain, 'fsdp', axis=0, tiled=False)  24.1 us
  transfers between devices with their start and end apart: 4, of which 4 were waited for; matrix products, arithmetic and copies ran while one was open for 5% of the time, Pallas kernels for 0%

profile of v1, /device:TPU:1, one launch (start us, length us, event | category | flops | bytes accessed | tf_op | source)
XLA Modules:
  0.0 524.1 jit_solution(11299679481191658599)
XLA Ops:
  7.2 0.0 copy-start
  7.2 0.0 copy-start.5
  7.2 0.0 reduce-scatter.5.cloned.1.call-start
  7.2 1.1 copy.18
  8.3 1.0 copy.19
  9.4 0.0 reduce-scatter.5.cloned.1.call-update
  9.4 0.0 all-gather.5.cloned.1.call-start
  10.1 95.1 %reduce-scatter.5.cloned.1.call-done = bf16[32,1024]{1,0:T(8,128)(2,1)} async-done(((bf16[1024,1024]{1,0:T(8,128)(2,1)}), bf16[32,1024]{1,0:T(8,128)(2,1)}) %reduce-scatter.5.cloned.1.call-update) | async-done | bytes 65552 | tf_op jit(solution)/shard_map/reduce_scatter | solution.py:42
  105.2 1.6 bitcast_subtract_fusion
  106.8 0.0 all-gather.5.cloned.1.call-update
  106.8 0.0 all-gather.7.cloned.1.call-start
  106.9 0.7 all-gather.7.cloned.1.call-update
  107.5 0.0 reduce-scatter.3.cloned.1.call-start
  107.6 3.1 fusion.2
  110.7 0.0 copy-done
  110.7 0.0 copy-done.5
  110.7 8.1 %convolution_convert_fusion = bf16[8192,512]{1,0:T(8,128)(2,1)} fusion(bf16[256,512]{1,0:T(8,128)(2,1)S(1)} %copy-done, bf16[256,8192]{1,0:T(8,128)(2,1)} %param.8, f32[8192]{0:T(1024)S(1)} %bitcast.32, f32[256]{0:T(256)S(1)} %add_rsqrt_fusion), kind=kOutput, calls=%fused_computation | convolution fusion | flops 2160066560 | bytes 12878848 | tf_op jit(solution)/shard_map/dot_general | solution.py:31
  118.9 0.0 reduce-scatter.3.cloned.1.call-update
  118.9 0.9 copy-done.2
  119.8 0.9 bitcast_dynamic-update-slice_fusion
  120.7 0.0 copy-start.3
  120.7 0.0 copy-start.4
  120.7 48.0 %all-gather.5.cloned.1.call-done = f32[1024,1024]{1,0:T(8,128)} async-done(((f32[32,1024]{1,0:T(8,128)}), f32[1024,1024]{1,0:T(8,128)}) %all-gather.5.cloned.1.call-update) | async-done | bytes 4194320 | tf_op jit(solution)/shard_map/all_gather | solution.py:48
  168.8 0.0 copy-done.1
  168.8 4.3 fusion.7
  173.1 165.6 %all-gather.7.cloned.1.call-done = bf16[1,8192,512]{2,1,0:T(8,128)(2,1)} async-done(((bf16[1,1024,512]{2,1,0:T(8,128)(2,1)}), bf16[1,8192,512]{2,1,0:T(8,128)(2,1)}) %all-gather.7.cloned.1.call-update) | async-done | bytes 8388624 | tf_op jit(solution)/shard_map/all_gather | solution.py:21
  338.6 7.0 %fusion.8 = f32[8192]{0:T(1024)S(1)} fusion(bf16[256,512]{1,0:T(8,128)(2,1)S(1)} %copy-done, bf16[1,8192,512]{2,1,0:T(8,128)(2,1)} %all-gather.7.cloned.1.call-done, f32[256]{0:T(256)S(1)} %add_rsqrt_fusion, bf16[256,8192]{1,0:T(8,128)(2,1)} %param.8), kind=kOutput, calls=%fused_computation.12 | convolution fusion | flops 2155864064 | bytes 12878848 | tf_op jit(solution)/shard_map/dot_general | solution.py:19
  345.6 0.0 copy-done.3
  345.6 24.1 %all-gather.1 = f32[65536]{0:T(1024)S(1)} all-gather(f32[8192]{0:T(1024)S(1)} %fusion.8), channel_id=3, replica_groups=mesh['replica'=32,'fsdp'=8] {'fsdp'}, dimensions={0}, use_global_device_ids=true | all-gather | bytes 294912 | tf_op jit(solution)/shard_map/all_gather | solution.py:27
  369.7 0.1 reshape.21
  369.7 0.7 reduce_sum.29
  370.4 147.1 %reduce-scatter.3.cloned.1.call-done = bf16[1024,512]{1,0:T(8,128)(2,1)} async-done(((bf16[8192,512]{1,0:T(8,128)(2,1)}), bf16[1024,512]{1,0:T(8,128)(2,1)}) %reduce-scatter.3.cloned.1.call-update) | async-done | bytes 1048592 | tf_op jit(solution)/shard_map/reduce_scatter | solution.py:30
  (4 shorter events, 0.0 us)
Async XLA Ops:
  7.2 103.5 %copy-start = (bf16[256,512]{1,0:T(8,128)(2,1)S(1)}, bf16[256,512]{1,0:T(8,128)(2,1)}, u32[]{:S(2)}) copy-start(bf16[256,512]{1,0:T(8,128)(2,1)} %param.9) | copy-start | bytes 786436
  7.2 103.5 %copy-start.5 = (f32[1,8192]{1,0:T(1,128)S(1)}, f32[1,8192]{1,0:T(1,128)}, u32[]{:S(2)}) copy-start(f32[1,8192]{1,0:T(1,128)} %param.10) | copy-start | bytes 98308
  7.2 98.0 %reduce-scatter.5.cloned.1.call-start = ((), (), s32[]{:S(2)}) async-start(), calls=%async_computation.3 | async-start | bytes 2162688 | tf_op jit(solution)/shard_map/reduce_scatter | solution.py:42
  9.4 159.4 %all-gather.5.cloned.1.call-start = ((), (), s32[]{:S(2)}) async-start(), calls=%async_computation.4 | async-start | bytes 4325376 | tf_op jit(solution)/shard_map/all_gather | solution.py:48
  106.8 231.8 %all-gather.7.cloned.1.call-start = ((), (), s32[]{:S(2)}) async-start(), calls=%async_computation.5 | async-start | bytes 9437184 | tf_op jit(solution)/shard_map/all_gather | solution.py:21
  107.5 410.0 %reduce-scatter.3.cloned.1.call-start = ((), (), s32[]{:S(2)}) async-start(), calls=%async_computation.2 | async-start | bytes 9437184 | tf_op jit(solution)/shard_map/reduce_scatter | solution.py:30
  118.9 0.9 copy-start.2
  118.9 49.9 %copy-start.1 = (bf16[1,1024,1024]{2,1,0:T(8,128)(2,1)S(1)}, bf16[1,1024,1024]{2,1,0:T(8,128)(2,1)}, u32[]{:S(2)}) copy-start(bf16[1,1024,1024]{2,1,0:T(8,128)(2,1)} %param.12) | copy-start | bytes 6291460
  120.7 224.9 %copy-start.3 = (f32[4,32,1024]{2,1,0:T(8,128)}, f32[4,32,1024]{2,1,0:T(8,128)S(1)}, u32[]{:S(2)}) copy-start(f32[4,32,1024]{2,1,0:T(8,128)S(1)} %get-tuple-element.8) | copy-start | bytes 1572868
  120.7 224.9 %copy-start.4 = (f32[4,32,1024]{2,1,0:T(8,128)}, f32[4,32,1024]{2,1,0:T(8,128)S(1)}, u32[]{:S(2)}) copy-start(f32[4,32,1024]{2,1,0:T(8,128)S(1)} %get-tuple-element.7) | copy-start | bytes 1572868
Sparse Core Ops, SparseCore 0:
  11.9 93.3 reduce-scatter.4
  108.3 60.3 all-gather.4
  170.6 167.9 all-gather.6
  341.6 175.9 reduce-scatter.2

commit v2 on v0

--- a/solution.py
+++ b/solution.py
@@ -1,3 +1,4 @@
+import functools
 import jax
 import jax.numpy as jnp
 from jax import lax
@@ -9,6 +10,18 @@
 mix_weight = 0.5
 
 
+def start_pools(payload, link_axis, dim_at):
+    return jnp.concatenate(
+        jax.lax.all_to_all(
+            jnp.stack([payload for _ in range(jax.lax.axis_size(link_axis))]), link_axis, 0, 0
+        ),
+        dim_at,
+    )
+
+
+wires_carry = functools.partial(start_pools, link_axis="fsdp", dim_at=0)
+
+
 def body(tokens, cotangent, gain, value_weight, fragment, global_table, momentum_table, frag_index):
     gains = gain[0]
     weight = value_weight[0]
@@ -17,10 +30,7 @@
     normed = floats * inverse
     scaled = (normed * gains).astype(jnp.bfloat16)
     back = lax.dot_general(
-        cotangent,
-        lax.all_gather(weight, "fsdp", axis=0, tiled=True),
-        (((1,), (1,)), ((), ())),
-        preferred_element_type=jnp.float32,
+        cotangent, wires_carry(weight), (((1,), (1,)), ((), ())), preferred_element_type=jnp.float32
     )
     columns = normed
     partial_gain = jnp.sum(columns * back, axis=0)

time: 522 us -> 408 us (0.78)
  waiting for transfers between devices: 452 us -> 318 us
  blocking collectives: 27.4 us -> 35.9 us
    all_gather x1 -> x0, waiting for transfers between devices: 166 us -> none  [body(): lax.all_gather(weight, 'fsdp', axis=0, tiled=True)]
    all_gather x1, waiting for transfers between devices: 48 us -> 203 us  [body(): full_params = lax.all_gather(new_params, 'replica', axis=0, tiled=True)]
    reduce_scatter x1, waiting for transfers between devices: 142 us -> 19.2 us  [body(): lax.psum_scatter(lax.dot_general(columns, cotangent, (((0,), (0,)), ((),...]
    psum x1, blocking collectives: 27.4 us -> 35.9 us  [body(): gain_grad = lax.psum(partial_gain, 'fsdp')]
  transfers between devices with their start and end apart: 4 -> 4, of which waited for: 4 -> 3; matrix products, arithmetic and copies ran while one was open for 4% -> 7% of each run, Pallas kernels for 0% -> 0%
where the time goes in v2:
time: 408 us
  waiting for transfers between devices  318 us (78%)
  blocking collectives  35.9 us (9%)
  between operations  16.2 us (4%)
  matrix products  15.2 us (4%)
  other arithmetic  8.97 us (2%)
  local copies, waits for them, and re-layouts  8.27 us (2%)
  starting transfers between devices  5.26 us (1%)
    all_gather x1, waiting for transfers between devices, body(): full_params = lax.all_gather(new_params, 'replica', axis=0, tiled=True)  203 us
    reduce_scatter x1, waiting for transfers between devices, body(): lax.psum_scatter(local.astype(jnp.bfloat16), 'replica', scatter_dimension...  95.1 us
    psum x1, blocking collectives, body(): gain_grad = lax.psum(partial_gain, 'fsdp')  35.9 us
    reduce_scatter x1, waiting for transfers between devices, body(): lax.psum_scatter(lax.dot_general(columns, cotangent, (((0,), (0,)), ((),...  19.2 us
    dot_general x1, matrix products, body(): lax.dot_general(columns, cotangent, (((0,), (0,)), ((), ())), preferred_e...  8.17 us
  transfers between devices with their start and end apart: 4, of which 3 were waited for; matrix products, arithmetic and copies ran while one was open for 7% of the time, Pallas kernels for 0%

profile of v2, /device:TPU:1, one launch (start us, length us, event | category | flops | bytes accessed | tf_op | source)
XLA Modules:
  0.0 407.7 jit_solution(17397073163510286047)
XLA Ops:
  8.0 0.0 copy-start
  8.0 0.0 copy-start.6
  8.0 0.0 reduce-scatter.5.cloned.1.call-start
  8.1 1.1 copy.18
  9.1 1.0 copy.19
  10.2 0.0 reduce-scatter.5.cloned.1.call-update
  10.2 0.0 all-gather.2.cloned.1.call-start
  10.9 95.1 %reduce-scatter.5.cloned.1.call-done = bf16[32,1024]{1,0:T(8,128)(2,1)} async-done(((bf16[1024,1024]{1,0:T(8,128)(2,1)}), bf16[32,1024]{1,0:T(8,128)(2,1)}) %reduce-scatter.5.cloned.1.call-update) | async-done | bytes 65552 | tf_op jit(solution)/shard_map/reduce_scatter | solution.py:51
  106.0 1.6 bitcast_subtract_fusion
  107.6 0.0 all-gather.2.cloned.1.call-update
  107.6 0.0 reduce-scatter.3.cloned.1.call-start
  107.7 3.1 fusion.2
  110.8 0.0 copy-done
  110.8 0.0 copy-done.6
  110.8 8.2 %convolution_convert_fusion = bf16[8192,512]{1,0:T(8,128)(2,1)} fusion(bf16[256,512]{1,0:T(8,128)(2,1)S(1)} %copy-done, bf16[256,8192]{1,0:T(8,128)(2,1)} %param.8, f32[8192]{0:T(1024)S(1)} %bitcast.31, f32[256]{0:T(256)S(1)} %add_rsqrt_fusion), kind=kOutput, calls=%fused_computation | convolution fusion | flops 2160066560 | bytes 12878848 | tf_op jit(solution)/shard_map/dot_general | solution.py:40
  119.0 0.0 reduce-scatter.3.cloned.1.call-update
  119.0 1.2 copy-done.3
  120.2 3.9 stack.3
  124.2 5.1 %all-to-all-start = ((bf16[8,1024,512]{2,1,0:T(8,128)(2,1)}), bf16[8,1024,512]{2,1,0:T(8,128)(2,1)}, u32[]{:S(2)}, u32[]{:S(2)}) async-start(bf16[8,1024,512]{2,1,0:T(8,128)(2,1)} %stack.3), calls=%async_computation.1 | async-start | bytes 16777216 | tf_op jit(solution)/shard_map/all_to_all | solution.py:15
  129.3 0.0 copy-done.2
  129.3 1.0 bitcast_dynamic-update-slice_fusion
  130.3 0.0 copy-start.4
  130.3 0.0 copy-start.5
  130.3 203.4 %all-gather.2.cloned.1.call-done = f32[1024,1024]{1,0:T(8,128)} async-done(((f32[32,1024]{1,0:T(8,128)}), f32[1024,1024]{1,0:T(8,128)}) %all-gather.2.cloned.1.call-update) | async-done | bytes 4194320 | tf_op jit(solution)/shard_map/all_gather | solution.py:57
  333.8 0.0 copy-done.1
  333.8 4.3 %fusion.6 = bf16[1,1024,1024]{2,1,0:T(8,128)(2,1)} fusion(f32[1024,1024]{1,0:T(8,128)} %all-gather.2.cloned.1.call-done, bf16[1,1024,1024]{2,1,0:T(8,128)(2,1)S(1)} %copy-done.1), kind=kLoop, calls=%fused_computation.10 | loop fusion | flops 4194304 | bytes 8388608 | tf_op jit(solution)/shard_map/broadcast_in_dim | solution.py:58
  338.0 0.0 all-to-all-done
  338.0 7.1 %fusion.7 = f32[8192]{0:T(1024)S(1)} fusion(bf16[256,512]{1,0:T(8,128)(2,1)S(1)} %copy-done, bf16[8192,512]{1,0:T(8,128)(2,1)} %bitcast.3, f32[256]{0:T(256)S(1)} %add_rsqrt_fusion, bf16[256,8192]{1,0:T(8,128)(2,1)} %param.8), kind=kOutput, calls=%fused_computation.11 | convolution fusion | flops 2155864064 | bytes 12878848 | tf_op jit(solution)/shard_map/dot_general | solution.py:32
  345.1 0.0 copy-done.4
  345.1 0.0 copy-done.5
  345.1 35.9 %psum.7 = f32[1,8192]{1,0:T(1,128)} all-reduce(f32[1,8192]{1,0:T(1,128)S(1)} %bitcast.29), channel_id=1, replica_groups=mesh['replica'=32,'fsdp'=8] {'fsdp'}, use_global_device_ids=true, to_apply=%region_3.0 | all-reduce | flops 8192 | bytes 65536 | tf_op jit(solution)/shard_map/psum | solution.py:37
  381.0 19.2 %reduce-scatter.3.cloned.1.call-done = bf16[1024,512]{1,0:T(8,128)(2,1)} async-done(((bf16[8192,512]{1,0:T(8,128)(2,1)}), bf16[1024,512]{1,0:T(8,128)(2,1)}) %reduce-scatter.3.cloned.1.call-update) | async-done | bytes 1048592 | tf_op jit(solution)/shard_map/reduce_scatter | solution.py:39
  (4 shorter events, 0.0 us)
Async XLA Ops:
  8.0 102.8 %copy-start = (bf16[256,512]{1,0:T(8,128)(2,1)S(1)}, bf16[256,512]{1,0:T(8,128)(2,1)}, u32[]{:S(2)}) copy-start(bf16[256,512]{1,0:T(8,128)(2,1)} %param.9) | copy-start | bytes 786436
  8.0 102.8 %copy-start.6 = (f32[1,8192]{1,0:T(1,128)S(1)}, f32[1,8192]{1,0:T(1,128)}, u32[]{:S(2)}) copy-start(f32[1,8192]{1,0:T(1,128)} %param.10) | copy-start | bytes 98308
  8.0 98.0 %reduce-scatter.5.cloned.1.call-start = ((), (), s32[]{:S(2)}) async-start(), calls=%async_computation.4 | async-start | bytes 2162688 | tf_op jit(solution)/shard_map/reduce_scatter | solution.py:51
  10.2 323.5 %all-gather.2.cloned.1.call-start = ((), (), s32[]{:S(2)}) async-start(), calls=%async_computation.5 | async-start | bytes 4325376 | tf_op jit(solution)/shard_map/all_gather | solution.py:57
  107.6 292.6 %reduce-scatter.3.cloned.1.call-start = ((), (), s32[]{:S(2)}) async-start(), calls=%async_computation.3 | async-start | bytes 9437184 | tf_op jit(solution)/shard_map/reduce_scatter | solution.py:39
  119.0 1.2 copy-start.3
  124.2 5.2 %copy-start.2 = (f32[32,1024]{1,0:T(8,128)S(1)}, f32[32,1024]{1,0:T(8,128)}, u32[]{:S(2)}) copy-start(f32[32,1024]{1,0:T(8,128)} %get-tuple-element.5) | copy-start | bytes 393220
  124.2 209.6 %copy-start.1 = (bf16[1,1024,1024]{2,1,0:T(8,128)(2,1)S(1)}, bf16[1,1024,1024]{2,1,0:T(8,128)(2,1)}, u32[]{:S(2)}) copy-start(bf16[1,1024,1024]{2,1,0:T(8,128)(2,1)} %param.12) | copy-start | bytes 6291460
  124.2 213.9 %all-to-all-start = ((bf16[8,1024,512]{2,1,0:T(8,128)(2,1)}), bf16[8,1024,512]{2,1,0:T(8,128)(2,1)}, u32[]{:S(2)}, u32[]{:S(2)}) async-start(bf16[8,1024,512]{2,1,0:T(8,128)(2,1)} %stack.3), calls=%async_computation.1 | async-start | bytes 16777216 | tf_op jit(solution)/shard_map/all_to_all | solution.py:15
  130.3 214.8 %copy-start.4 = (f32[4,32,1024]{2,1,0:T(8,128)}, f32[4,32,1024]{2,1,0:T(8,128)S(1)}, u32[]{:S(2)}) copy-start(f32[4,32,1024]{2,1,0:T(8,128)S(1)} %get-tuple-element.8) | copy-start | bytes 1572868
  130.3 214.8 %copy-start.5 = (f32[4,32,1024]{2,1,0:T(8,128)}, f32[4,32,1024]{2,1,0:T(8,128)S(1)}, u32[]{:S(2)}) copy-start(f32[4,32,1024]{2,1,0:T(8,128)S(1)} %get-tuple-element.7) | copy-start | bytes 1572868
Sparse Core Ops, SparseCore 0:
  12.7 93.3 reduce-scatter.4
  109.2 224.5 all-gather.1
Sparse Core Ops, SparseCore 1:
  119.1 281.1 reduce-scatter.2
